TPU v7x, 128 devices: a whole 4x4x4 slice. The times are simulated.
128 devices in a mesh: sec: 32 (over z, x, core), col: 4 (over y).
Axes of the slice: x: 4, y: 4, z: 4, core: 2. Of those that a mesh axis runs over, the one named last changes fastest.
Arguments:
- right_sides: float32 [32, 4, 20, 128, 256], P('sec', 'col'), may hold values from -6 to 6
- diag_inverse: float32 [32, 4, 20, 128, 128], P('sec', 'col'), may hold values from -1 to 1
- coupling: float32 [32, 4, 20, 128, 128], P('sec', 'col'), may hold values from -1 to 1
- off_blocks: float32 [32, 4, 15, 16, 128, 128], P('sec', 'col'), may hold values from -0.125 to 0.125
- pattern: int32 [32, 4, 15, 16], P('sec', 'col'), may hold values from 0 to 59, as said below
Outputs:
- solution: float32 [32, 4, 20, 128, 256], P('sec', 'col')
Inputs may be any that keep to these rules, and one draw needn't show every extreme that they name: `pattern`: in a device's list, entry (l - 1) * 5 + k holds 16 different positions below l * 4 * 5, that is of levels under l.
All inputs are finite; a program needn't handle non-finite values.
Results may differ from a plain program's by a relative error of at most 0.0003.
Values sent between devices are 32-bit elements; how exact they have to be, the bound alone decides.
A program may use at most 128 MiB of HBM per device.

v0:
```python
import jax
import jax.numpy as jnp
from jax import lax
from jax.sharding import PartitionSpec as P

LEV = 4


HIGH = lax.Precision.HIGHEST


def passed_along(value, axis, steps):
    count = lax.axis_size(axis)
    first, last = (max(0, -steps), min(count, count - steps))
    return lax.ppermute(value, axis, [(source, source + steps) for source in range(first, last)])


def per_device(right_sides, diag_inverse, coupling, off_blocks, pattern):
    right_sides = right_sides[0, 0]
    diag_inverse = diag_inverse[0, 0]
    coupling = coupling[0, 0]
    off_blocks = off_blocks[0, 0]
    pattern = pattern[0, 0]
    row_count = right_sides.shape[0]
    block_order = right_sides.shape[1]
    rhs_columns = right_sides.shape[2]
    per_level = row_count // LEV
    col_count = lax.axis_size("col")
    stacked = jnp.concatenate([right_sides, -coupling], axis=2)
    section_table = jnp.zeros(
        (col_count * row_count, block_order, rhs_columns + block_order), jnp.float32
    )
    own_solved = []
    for level_index in range(LEV):
        first_row = level_index * per_level
        current = stacked[first_row : first_row + per_level]
        if level_index > 0:
            lower_row = (level_index - 1) * per_level
            picked = jnp.take(section_table, pattern[lower_row : lower_row + per_level], axis=0)
            current = current - jnp.einsum(
                "pkab,pkbw->paw",
                off_blocks[lower_row : lower_row + per_level],
                picked,
                precision=HIGH,
            )
        solved = jnp.einsum(
            "pab,pbw->paw", diag_inverse[first_row : first_row + per_level], current, precision=HIGH
        )
        own_solved.append(solved)
        shared = lax.all_gather(solved, "col", axis=0, tiled=True)
        start_row = level_index * col_count * per_level
        section_table = section_table.at[start_row : start_row + col_count * per_level].set(shared)
    boundary = section_table[-1]
    carry_base = boundary[:, :rhs_columns]
    carry_map = boundary[:, rhs_columns:]
    sec_count = lax.axis_size("sec")

    def relay_step(step_index, previous):
        advanced = carry_base + jnp.dot(carry_map, previous, precision=HIGH)
        return passed_along(advanced, "sec", 1)

    previous = lax.fori_loop(0, sec_count - 1, relay_step, jnp.zeros_like(carry_base))
    solution = jnp.concatenate(own_solved, axis=0)
    result = solution[:, :, :rhs_columns] + jnp.einsum(
        "pab,bw->paw", solution[:, :, rhs_columns:], previous, precision=HIGH
    )
    return result[None, None]


def solution(mesh):
    return jax.shard_map(
        per_device,
        mesh=mesh,
        in_specs=(
            P("sec", "col", None, None, None),
            P("sec", "col", None, None, None),
            P("sec", "col", None, None, None),
            P("sec", "col", None, None, None, None),
            P("sec", "col", None, None),
        ),
        out_specs=P("sec", "col", None, None, None),
        check_vma=False,
    )
```

profile of v0, /device:TPU:32, one launch (start us, length us, event | category | flops | bytes accessed | tf_op | source)
XLA Modules:
  0.0 674.6 jit_solution(5097712981208865047)
XLA Ops:
  19.5 48.1 %all-gather.5.cloned.1.call-done = f32[20,128,384]{2,1,0:T(8,128)} async-done(((f32[5,128,384]{2,1,0:T(8,128)}), f32[20,128,384]{2,1,0:T(8,128)}) %all-gather.5.cloned.1.call-update) | async-done | bytes 3932176 | tf_op jit(solution)/shard_map/all_gather | solution.py:50
  67.6 9.5 %scatter.10 = f32[80,128,384]{2,1,0:T(8,128)} pad(f32[20,128,384]{2,1,0:T(8,128)} %all-gather.5.cloned.1.call-done, f32[]{:T(128)} %constant.123.clone.1), padding=0_60x0_0x0_0 | pad | bytes 19660804 | tf_op jit(solution)/shard_map/scatter | solution.py:52
  77.1 19.7 %gather_fusion = f32[80,128,384]{2,1,0:T(8,128)} fusion(f32[80,128,384]{2,1,0:T(8,128)} %scatter.10, s32[1024]{0:T(1024)S(1)} %pad_clamp_fusion.2), kind=kCustom, calls=%fused_computation.clone | custom fusion | bytes 31457600 | tf_op jit(solution)/shard_map/jit(_take)/gather | solution.py:39
  96.9 29.6 %fusion.51 = f32[5,128,384]{1,2,0:T(8,128)S(1)} fusion(f32[1,1,15,16,128,128]{5,4,3,2,1,0:T(8,128)} %param.20, f32[5,16,128,384]{3,2,1,0:T(8,128)} %bitcast.107, pred[5,16]{1,0:T(8,128)(4,1)S(1)} %compare_and_fusion.2, f32[20,128,128]{1,2,0:T(8,128)} %copy-done, f32[20,128,256]{1,2,0:T(8,128)S(1)} %bitcast.103), kind=kOutput, calls=%fused_computation.38 | convolution fusion | flops 6044221440 | bytes 25886800 | tf_op jit(solution)/shard_map/pkab,pkbw->paw/dot_general | solution.py:40
  132.3 46.3 %all-gather.7.cloned.1.call-done = f32[20,128,384]{2,1,0:T(8,128)} async-done(((f32[5,128,384]{2,1,0:T(8,128)}), f32[20,128,384]{2,1,0:T(8,128)}) %all-gather.7.cloned.1.call-update) | async-done | bytes 3932176 | tf_op jit(solution)/shard_map/all_gather | solution.py:50
  183.0 19.0 %gather_fusion.1 = f32[80,128,384]{2,1,0:T(8,128)} fusion(f32[80,128,384]{2,1,0:T(8,128)} %constant_dynamic-update-slice_fusion.1, s32[1024]{0:T(1024)S(1)} %pad_clamp_fusion.1), kind=kCustom, calls=%fused_computation.1.clone | custom fusion | bytes 31457600 | tf_op jit(solution)/shard_map/jit(_take)/gather | solution.py:39
  202.0 29.7 %fusion.46 = f32[5,128,384]{1,2,0:T(8,128)S(1)} fusion(f32[1,1,15,16,128,128]{5,4,3,2,1,0:T(8,128)} %param.20, f32[5,16,128,384]{3,2,1,0:T(8,128)} %bitcast.108, pred[5,16]{1,0:T(8,128)(4,1)S(1)} %get-tuple-element.95, f32[20,128,128]{1,2,0:T(8,128)} %copy-done, f32[20,128,256]{1,2,0:T(8,128)S(1)} %bitcast.104), kind=kOutput, calls=%fused_computation.37 | convolution fusion | flops 6044221440 | bytes 25886800 | tf_op jit(solution)/shard_map/pkab,pkbw->paw/dot_general | solution.py:40
  237.5 46.2 %all-gather.9.cloned.1.call-done = f32[20,128,384]{2,1,0:T(8,128)} async-done(((f32[5,128,384]{2,1,0:T(8,128)}), f32[20,128,384]{2,1,0:T(8,128)}) %all-gather.9.cloned.1.call-update) | async-done | bytes 3932176 | tf_op jit(solution)/shard_map/all_gather | solution.py:50
  288.1 18.6 %gather_fusion.2 = f32[80,128,384]{2,1,0:T(8,128)} fusion(f32[80,128,384]{2,1,0:T(8,128)} %constant_dynamic-update-slice_fusion, s32[1024]{0:T(1024)S(1)} %pad_clamp_fusion), kind=kCustom, calls=%fused_computation.2.clone | custom fusion | bytes 31457600 | tf_op jit(solution)/shard_map/jit(_take)/gather | solution.py:39
  306.7 29.9 %fusion.41 = f32[5,128,384]{1,2,0:T(8,128)S(1)} fusion(f32[1,1,15,16,128,128]{5,4,3,2,1,0:T(8,128)} %param.20, f32[5,16,128,384]{3,2,1,0:T(8,128)} %bitcast.106, pred[5,16]{1,0:T(8,128)(4,1)S(1)} %get-tuple-element.94, f32[20,128,128]{1,2,0:T(8,128)} %copy-done, f32[20,128,256]{1,2,0:T(8,128)S(1)} %bitcast.105), kind=kOutput, calls=%fused_computation.36 | convolution fusion | flops 6044221440 | bytes 25886800 | tf_op jit(solution)/shard_map/pkab,pkbw->paw/dot_general | solution.py:40
  346.0 43.3 %all-gather.11.cloned.1.call-done = f32[20,128,384]{2,1,0:T(8,128)} async-done(((f32[5,128,384]{2,1,0:T(8,128)}), f32[20,128,384]{2,1,0:T(8,128)}) %all-gather.11.cloned.1.call-update) | async-done | bytes 3932176 | tf_op jit(solution)/shard_map/all_gather | solution.py:50
  390.2 268.6 %while.14 = (s32[]{:T(128)}, f32[128,256]{1,0:T(8,128)S(1)}, f32[128,128]{1,0:T(8,128)S(1)}, f32[128,256]{1,0:T(8,128)S(1)}, s32[]{:T(128)}) while((s32[]{:T(128)}, f32[128,256]{1,0:T(8,128)S(1)}, f32[128,128]{1,0:T(8,128)S(1)}, f32[128,256]{1,0:T(8,128)S(1)}, s32[]{:T(128)}) %tuple.40), condition=%wide.region_1.0_spmd, body=%wide.region_0.2_spmd.sunk | while | flops 50364416 | bytes 983141 | solution.py:62
  392.4 6.5 collective-permute-done
  409.8 6.5 collective-permute-done
  418.4 6.5 collective-permute-done
  427.1 6.5 collective-permute-done
  435.7 6.5 collective-permute-done
  470.4 6.5 collective-permute-done
  479.1 6.5 collective-permute-done
  487.7 6.5 collective-permute-done
  505.1 6.5 collective-permute-done
  522.4 6.5 collective-permute-done
  539.7 6.5 collective-permute-done
  557.1 6.5 collective-permute-done
  (128 shorter events, 242.9 us)
Async XLA Ops:
  6.5 61.1 %all-gather.5.cloned.1.call-start = ((), (), s32[]{:S(2)}) async-start(), calls=%async_computation | async-start | bytes 4915200 | tf_op jit(solution)/shard_map/all_gather | solution.py:50
  19.3 159.3 %all-gather.7.cloned.1.call-start = ((), (), s32[]{:S(2)}) async-start(), calls=%async_computation.1 | async-start | bytes 4915200 | tf_op jit(solution)/shard_map/all_gather | solution.py:50
  131.9 151.8 %all-gather.9.cloned.1.call-start = ((), (), s32[]{:S(2)}) async-start(), calls=%async_computation.2 | async-start | bytes 4915200 | tf_op jit(solution)/shard_map/all_gather | solution.py:50
  237.2 152.1 %all-gather.11.cloned.1.call-start = ((), (), s32[]{:S(2)}) async-start(), calls=%async_computation.3 | async-start | bytes 4915200 | tf_op jit(solution)/shard_map/all_gather | solution.py:50
  390.5 8.4 %collective-permute-start = (f32[128,256]{1,0:T(8,128)S(1)}, f32[128,256]{1,0:T(8,128)S(1)}, u32[]{:S(2)}, u32[]{:S(2)}) collective-permute-start(f32[128,256]{1,0:T(8,128)S(1)} %convolution_add_fusion.2), channel_id=1, source_target_pairs={{0,4},{4,8},{8,12},{12,16},{16,20},{20,24},{24,28},{28,32},{32,36}... | collective-permute-start | bytes 393224 | tf_op jit(solution)/shard_map/while/body/eval_jaxpr/ppermute | solution.py:15
  399.2 8.4 %collective-permute-start = (f32[128,256]{1,0:T(8,128)S(1)}, f32[128,256]{1,0:T(8,128)S(1)}, u32[]{:S(2)}, u32[]{:S(2)}) collective-permute-start(f32[128,256]{1,0:T(8,128)S(1)} %convolution_add_fusion.2), channel_id=1, source_target_pairs={{0,4},{4,8},{8,12},{12,16},{16,20},{20,24},{24,28},{28,32},{32,36}... | collective-permute-start | bytes 393224 | tf_op jit(solution)/shard_map/while/body/eval_jaxpr/ppermute | solution.py:15
  407.8 8.4 %collective-permute-start = (f32[128,256]{1,0:T(8,128)S(1)}, f32[128,256]{1,0:T(8,128)S(1)}, u32[]{:S(2)}, u32[]{:S(2)}) collective-permute-start(f32[128,256]{1,0:T(8,128)S(1)} %convolution_add_fusion.2), channel_id=1, source_target_pairs={{0,4},{4,8},{8,12},{12,16},{16,20},{20,24},{24,28},{28,32},{32,36}... | collective-permute-start | bytes 393224 | tf_op jit(solution)/shard_map/while/body/eval_jaxpr/ppermute | solution.py:15
  416.5 8.4 %collective-permute-start = (f32[128,256]{1,0:T(8,128)S(1)}, f32[128,256]{1,0:T(8,128)S(1)}, u32[]{:S(2)}, u32[]{:S(2)}) collective-permute-start(f32[128,256]{1,0:T(8,128)S(1)} %convolution_add_fusion.2), channel_id=1, source_target_pairs={{0,4},{4,8},{8,12},{12,16},{16,20},{20,24},{24,28},{28,32},{32,36}... | collective-permute-start | bytes 393224 | tf_op jit(solution)/shard_map/while/body/eval_jaxpr/ppermute | solution.py:15
  425.1 8.4 %collective-permute-start = (f32[128,256]{1,0:T(8,128)S(1)}, f32[128,256]{1,0:T(8,128)S(1)}, u32[]{:S(2)}, u32[]{:S(2)}) collective-permute-start(f32[128,256]{1,0:T(8,128)S(1)} %convolution_add_fusion.2), channel_id=1, source_target_pairs={{0,4},{4,8},{8,12},{12,16},{16,20},{20,24},{24,28},{28,32},{32,36}... | collective-permute-start | bytes 393224 | tf_op jit(solution)/shard_map/while/body/eval_jaxpr/ppermute | solution.py:15
  433.8 8.4 %collective-permute-start = (f32[128,256]{1,0:T(8,128)S(1)}, f32[128,256]{1,0:T(8,128)S(1)}, u32[]{:S(2)}, u32[]{:S(2)}) collective-permute-start(f32[128,256]{1,0:T(8,128)S(1)} %convolution_add_fusion.2), channel_id=1, source_target_pairs={{0,4},{4,8},{8,12},{12,16},{16,20},{20,24},{24,28},{28,32},{32,36}... | collective-permute-start | bytes 393224 | tf_op jit(solution)/shard_map/while/body/eval_jaxpr/ppermute | solution.py:15
  451.1 8.4 %collective-permute-start = (f32[128,256]{1,0:T(8,128)S(1)}, f32[128,256]{1,0:T(8,128)S(1)}, u32[]{:S(2)}, u32[]{:S(2)}) collective-permute-start(f32[128,256]{1,0:T(8,128)S(1)} %convolution_add_fusion.2), channel_id=1, source_target_pairs={{0,4},{4,8},{8,12},{12,16},{16,20},{20,24},{24,28},{28,32},{32,36}... | collective-permute-start | bytes 393224 | tf_op jit(solution)/shard_map/while/body/eval_jaxpr/ppermute | solution.py:15
  468.5 8.4 %collective-permute-start = (f32[128,256]{1,0:T(8,128)S(1)}, f32[128,256]{1,0:T(8,128)S(1)}, u32[]{:S(2)}, u32[]{:S(2)}) collective-permute-start(f32[128,256]{1,0:T(8,128)S(1)} %convolution_add_fusion.2), channel_id=1, source_target_pairs={{0,4},{4,8},{8,12},{12,16},{16,20},{20,24},{24,28},{28,32},{32,36}... | collective-permute-start | bytes 393224 | tf_op jit(solution)/shard_map/while/body/eval_jaxpr/ppermute | solution.py:15
  477.1 8.4 %collective-permute-start = (f32[128,256]{1,0:T(8,128)S(1)}, f32[128,256]{1,0:T(8,128)S(1)}, u32[]{:S(2)}, u32[]{:S(2)}) collective-permute-start(f32[128,256]{1,0:T(8,128)S(1)} %convolution_add_fusion.2), channel_id=1, source_target_pairs={{0,4},{4,8},{8,12},{12,16},{16,20},{20,24},{24,28},{28,32},{32,36}... | collective-permute-start | bytes 393224 | tf_op jit(solution)/shard_map/while/body/eval_jaxpr/ppermute | solution.py:15
  485.8 8.4 %collective-permute-start = (f32[128,256]{1,0:T(8,128)S(1)}, f32[128,256]{1,0:T(8,128)S(1)}, u32[]{:S(2)}, u32[]{:S(2)}) collective-permute-start(f32[128,256]{1,0:T(8,128)S(1)} %convolution_add_fusion.2), channel_id=1, source_target_pairs={{0,4},{4,8},{8,12},{12,16},{16,20},{20,24},{24,28},{28,32},{32,36}... | collective-permute-start | bytes 393224 | tf_op jit(solution)/shard_map/while/body/eval_jaxpr/ppermute | solution.py:15
  503.1 8.4 %collective-permute-start = (f32[128,256]{1,0:T(8,128)S(1)}, f32[128,256]{1,0:T(8,128)S(1)}, u32[]{:S(2)}, u32[]{:S(2)}) collective-permute-start(f32[128,256]{1,0:T(8,128)S(1)} %convolution_add_fusion.2), channel_id=1, source_target_pairs={{0,4},{4,8},{8,12},{12,16},{16,20},{20,24},{24,28},{28,32},{32,36}... | collective-permute-start | bytes 393224 | tf_op jit(solution)/shard_map/while/body/eval_jaxpr/ppermute | solution.py:15
  520.5 8.4 %collective-permute-start = (f32[128,256]{1,0:T(8,128)S(1)}, f32[128,256]{1,0:T(8,128)S(1)}, u32[]{:S(2)}, u32[]{:S(2)}) collective-permute-start(f32[128,256]{1,0:T(8,128)S(1)} %convolution_add_fusion.2), channel_id=1, source_target_pairs={{0,4},{4,8},{8,12},{12,16},{16,20},{20,24},{24,28},{28,32},{32,36}... | collective-permute-start | bytes 393224 | tf_op jit(solution)/shard_map/while/body/eval_jaxpr/ppermute | solution.py:15
  537.8 8.4 %collective-permute-start = (f32[128,256]{1,0:T(8,128)S(1)}, f32[128,256]{1,0:T(8,128)S(1)}, u32[]{:S(2)}, u32[]{:S(2)}) collective-permute-start(f32[128,256]{1,0:T(8,128)S(1)} %convolution_add_fusion.2), channel_id=1, source_target_pairs={{0,4},{4,8},{8,12},{12,16},{16,20},{20,24},{24,28},{28,32},{32,36}... | collective-permute-start | bytes 393224 | tf_op jit(solution)/shard_map/while/body/eval_jaxpr/ppermute | solution.py:15
  555.1 8.4 %collective-permute-start = (f32[128,256]{1,0:T(8,128)S(1)}, f32[128,256]{1,0:T(8,128)S(1)}, u32[]{:S(2)}, u32[]{:S(2)}) collective-permute-start(f32[128,256]{1,0:T(8,128)S(1)} %convolution_add_fusion.2), channel_id=1, source_target_pairs={{0,4},{4,8},{8,12},{12,16},{16,20},{20,24},{24,28},{28,32},{32,36}... | collective-permute-start | bytes 393224 | tf_op jit(solution)/shard_map/while/body/eval_jaxpr/ppermute | solution.py:15
  572.5 8.4 %collective-permute-start = (f32[128,256]{1,0:T(8,128)S(1)}, f32[128,256]{1,0:T(8,128)S(1)}, u32[]{:S(2)}, u32[]{:S(2)}) collective-permute-start(f32[128,256]{1,0:T(8,128)S(1)} %convolution_add_fusion.2), channel_id=1, source_target_pairs={{0,4},{4,8},{8,12},{12,16},{16,20},{20,24},{24,28},{28,32},{32,36}... | collective-permute-start | bytes 393224 | tf_op jit(solution)/shard_map/while/body/eval_jaxpr/ppermute | solution.py:15
  589.8 8.4 %collective-permute-start = (f32[128,256]{1,0:T(8,128)S(1)}, f32[128,256]{1,0:T(8,128)S(1)}, u32[]{:S(2)}, u32[]{:S(2)}) collective-permute-start(f32[128,256]{1,0:T(8,128)S(1)} %convolution_add_fusion.2), channel_id=1, source_target_pairs={{0,4},{4,8},{8,12},{12,16},{16,20},{20,24},{24,28},{28,32},{32,36}... | collective-permute-start | bytes 393224 | tf_op jit(solution)/shard_map/while/body/eval_jaxpr/ppermute | solution.py:15
  607.1 8.4 %collective-permute-start = (f32[128,256]{1,0:T(8,128)S(1)}, f32[128,256]{1,0:T(8,128)S(1)}, u32[]{:S(2)}, u32[]{:S(2)}) collective-permute-start(f32[128,256]{1,0:T(8,128)S(1)} %convolution_add_fusion.2), channel_id=1, source_target_pairs={{0,4},{4,8},{8,12},{12,16},{16,20},{20,24},{24,28},{28,32},{32,36}... | collective-permute-start | bytes 393224 | tf_op jit(solution)/shard_map/while/body/eval_jaxpr/ppermute | solution.py:15
  624.5 8.4 %collective-permute-start = (f32[128,256]{1,0:T(8,128)S(1)}, f32[128,256]{1,0:T(8,128)S(1)}, u32[]{:S(2)}, u32[]{:S(2)}) collective-permute-start(f32[128,256]{1,0:T(8,128)S(1)} %convolution_add_fusion.2), channel_id=1, source_target_pairs={{0,4},{4,8},{8,12},{12,16},{16,20},{20,24},{24,28},{28,32},{32,36}... | collective-permute-start | bytes 393224 | tf_op jit(solution)/shard_map/while/body/eval_jaxpr/ppermute | solution.py:15
  641.8 8.4 %collective-permute-start = (f32[128,256]{1,0:T(8,128)S(1)}, f32[128,256]{1,0:T(8,128)S(1)}, u32[]{:S(2)}, u32[]{:S(2)}) collective-permute-start(f32[128,256]{1,0:T(8,128)S(1)} %convolution_add_fusion.2), channel_id=1, source_target_pairs={{0,4},{4,8},{8,12},{12,16},{16,20},{20,24},{24,28},{28,32},{32,36}... | collective-permute-start | bytes 393224 | tf_op jit(solution)/shard_map/while/body/eval_jaxpr/ppermute | solution.py:15
  650.4 8.4 %collective-permute-start = (f32[128,256]{1,0:T(8,128)S(1)}, f32[128,256]{1,0:T(8,128)S(1)}, u32[]{:S(2)}, u32[]{:S(2)}) collective-permute-start(f32[128,256]{1,0:T(8,128)S(1)} %convolution_add_fusion.2), channel_id=1, source_target_pairs={{0,4},{4,8},{8,12},{12,16},{16,20},{20,24},{24,28},{28,32},{32,36}... | collective-permute-start | bytes 393224 | tf_op jit(solution)/shard_map/while/body/eval_jaxpr/ppermute | solution.py:15
  (15 other events, 110.1 us)
Sparse Core Ops, SparseCore 0:
  19.5 48.1 all-gather.4
  132.1 46.5 all-gather.6
  237.3 46.3 all-gather.8
  342.3 46.8 all-gather.10
where the time goes:
time: 679 us; the launch traced here: 675 us
  waiting for transfers between devices  384 us (57%)
  matrix products  115 us (17%)
  local copies, waits for them, and re-layouts  96.1 us (14%)
  starting transfers between devices  60 us (9%)
  between operations  13.6 us (2%)
    ppermute x31, waiting for transfers between devices, passed_along(): lax.ppermute(value, axis, [(source, source + steps) for source in range(f...  200 us
    all_gather x4, waiting for transfers between devices, per_device(): shared = lax.all_gather(solved, 'col', axis=0, tiled=True)  184 us
    dot_general x3, matrix products, per_device(): jnp.einsum('pkab,pkbw->paw', off_blocks[lower_row:lower_row + per_level],...  89.2 us
    ppermute x31, starting transfers between devices, passed_along(): lax.ppermute(value, axis, [(source, source + steps) for source in range(f...  59.5 us
    gather x3, local copies, waits for them, and re-layouts, per_device(): jnp.take(section_table, pattern[lower_row:lower_row + per_level], axis=0)  57.4 us
    scatter x3, local copies, waits for them, and re-layouts, per_device(): section_table.at[start_row:start_row + col_count * per_level].set(shared)  18.3 us
  transfers between devices with their start and end apart: 35, of which 35 were waited for; matrix products, arithmetic and copies ran while one was open for 1% of the time, Pallas kernels for 0%

commit v1 on v0

v1 whole, which is shorter than its diff:
```python
import functools

import jax
import jax.numpy as jnp
from jax import lax
from jax.experimental import pallas as pl
from jax.experimental.pallas import tpu as pltpu
from jax.sharding import PartitionSpec as P

LEV = 4
CHUNKS = 3
MESH = pl.DeviceIdType.MESH
F32 = jnp.float32
BF16 = jnp.bfloat16


def split(value):
    high = value.astype(BF16)
    return high, (value - high.astype(F32)).astype(BF16)


def dot(left, right):
    return jnp.dot(left, right, preferred_element_type=F32)


def dot3(left, right):
    left_high, left_low = split(left)
    right_high, right_low = split(right)
    both = dot(left_high, jnp.concatenate([right_high, right_low], axis=1))
    width = right.shape[1]
    return both[:, :width] + both[:, width:] + dot(left_low, right_high)


def section_kernel(
    pattern, right_sides, diag, coupling, off,
    y_out, w_out,
    rhs_v, diag_v, coup_v, off_v, got, table, top, in_sem, out_sem, send_sem, recv_sem,
):
    me = lax.axis_index("col")
    right, left, across = lax.rem(me + 1, 4), lax.rem(me + 3, 4), lax.rem(me + 2, 4)
    per_level = diag_v.shape[0] // LEV
    bs = diag_v.shape[1]
    half = per_level * bs // 2
    items = (LEV - 1) * CHUNKS

    def level_rows(level):
        return pl.ds(level * per_level, per_level)

    loads = []
    for level in range(LEV):
        rows = level_rows(level)
        parts = [(coupling.at[rows], coup_v.at[rows]), (diag.at[rows], diag_v.at[rows]), (right_sides.at[rows], rhs_v.at[rows])]
        if level:
            lower = level_rows(level - 1)
            parts.append((off.at[lower], off_v.at[lower]))
        loads.append([pltpu.make_async_copy(a, b, in_sem.at[level, i]) for i, (a, b) in enumerate(parts)])
    for group in loads:
        for copy in group:
            copy.start()

    barrier = pltpu.get_barrier_semaphore()
    for neighbour in (left, right):
        pl.semaphore_signal(barrier, inc=1, device_id={"col": neighbour}, device_id_type=MESH)

    lo, hi = pl.ds(0, half), pl.ds(half, half)

    def remote(item, slot, rows, index, target):
        ref = got.at[item, slot, rows]
        return pltpu.make_async_remote_copy(
            src_ref=ref, dst_ref=ref, send_sem=send_sem.at[item, index], recv_sem=recv_sem.at[item, index],
            device_id={"col": target}, device_id_type=MESH,
        )

    def own_sends(item):
        return [remote(item, me, lo, 0, right), remote(item, me, hi, 1, left), remote(item, me, hi, 2, right), remote(item, me, lo, 3, left)]

    def forwards(item):
        return [remote(item, left, lo, 4, right), remote(item, right, hi, 5, left)]

    def arrival(item, index):
        slot = (left, right, left, right, across, across)[index]
        return remote(item, slot, (lo, hi, hi, lo, lo, hi)[index], index, right)

    def forward(item):
        arrival(item, 0).wait_recv()
        go = forwards(item)
        go[0].start()
        arrival(item, 1).wait_recv()
        go[1].start()

    def finish(item):
        for index in range(2, 6):
            arrival(item, index).wait_recv()

    def to_table(level, chunk):
        item = level * CHUNKS + chunk
        base = chunk * (LEV - 1) * 4 * per_level + level * 4 * per_level

        def body(k, carry):
            for source in range(4):
                high, low = split(got[item, source, pl.ds(pl.multiple_of(k * bs, bs), bs), :])
                table[base + source * per_level + k, :, :bs] = high
                table[base + source * per_level + k, :, bs:] = low
            return carry

        lax.fori_loop(0, per_level, body, 0)

    def compute(level, chunk):
        def body(k, carry):
            row = level * per_level + k
            if chunk == 0:
                current = -coup_v[row]
            else:
                current = rhs_v[row, :, (chunk - 1) * bs : chunk * bs]
            if level:
                low_row = (level - 1) * per_level + k
                wide = jnp.zeros((bs, 2 * bs), F32)
                narrow = jnp.zeros((bs, bs), F32)
                base = chunk * (LEV - 1) * 4 * per_level
                for first in range(0, 16, 4):
                    pieces = [split(off_v[low_row, j]) for j in range(first, first + 4)]
                    picked = jnp.concatenate([table[base + pattern[low_row, j]] for j in range(first, first + 4)], axis=0)
                    wide += dot(jnp.concatenate([p[0] for p in pieces], axis=1), picked)
                    narrow += dot(jnp.concatenate([p[1] for p in pieces], axis=1), picked[:, :bs])
                current = current - (wide[:, :bs] + wide[:, bs:] + narrow)
            solved = dot3(diag_v[row], current)
            if level < LEV - 1:
                got[level * CHUNKS + chunk, me, pl.ds(pl.multiple_of(k * bs, bs), bs), :] = solved
            else:
                top[chunk, pl.ds(pl.multiple_of(k * bs, bs), bs), :] = solved
            return carry

        lax.fori_loop(0, per_level, body, 0)

    def writes(level, chunk):
        source = got.at[level * CHUNKS + chunk, me] if level < LEV - 1 else top.at[chunk]
        copies = []
        for k in range(per_level):
            row = level * per_level + k
            target = w_out.at[row] if chunk == 0 else y_out.at[row, :, pl.ds((chunk - 1) * bs, bs)]
            copies.append(pltpu.make_async_copy(source.at[pl.ds(k * bs, bs)], target, out_sem.at[level * CHUNKS + chunk, k]))
        return copies

    for copy in loads[0]:
        copy.wait()
    compute(0, 0)
    pl.semaphore_wait(barrier, 2)
    for item in range(items):
        for copy in own_sends(item):
            copy.start()
        for copy in writes(item // CHUNKS, item % CHUNKS):
            copy.start()
        following = item + 1
        if following < items:
            level, chunk = following // CHUNKS, following % CHUNKS
            if level:
                if chunk == 0:
                    for copy in loads[level]:
                        copy.wait()
                finish(following - CHUNKS)
                to_table(level - 1, chunk)
            compute(level, chunk)
        forward(item)
    for copy in loads[LEV - 1]:
        copy.wait()
    for chunk in range(CHUNKS):
        finish(items - CHUNKS + chunk)
        to_table(LEV - 2, chunk)
        compute(LEV - 1, chunk)
        for copy in writes(LEV - 1, chunk):
            copy.start()
    for item in range(items):
        for copy in own_sends(item) + forwards(item):
            copy.wait_send()
    for item in range(LEV * CHUNKS):
        for copy in writes(item // CHUNKS, item % CHUNKS):
            copy.wait()


def section_solve(right_sides, diag_inverse, coupling, off_blocks, pattern):
    rows, bs, width = right_sides.shape
    per_level = rows // LEV
    items = (LEV - 1) * CHUNKS
    any_space = pl.BlockSpec(memory_space=pl.ANY)
    return pl.pallas_call(
        section_kernel,
        out_shape=(jax.ShapeDtypeStruct((rows, bs, width), F32), jax.ShapeDtypeStruct((rows, bs, bs), F32)),
        in_specs=[pl.BlockSpec(memory_space=pltpu.SMEM)] + [any_space] * 4,
        out_specs=(any_space, any_space),
        scratch_shapes=[
            pltpu.VMEM((rows, bs, width), F32),
            pltpu.VMEM((rows, bs, bs), F32),
            pltpu.VMEM((rows, bs, bs), F32),
            pltpu.VMEM(off_blocks.shape, F32),
            pltpu.VMEM((items, 4, per_level * bs, bs), F32),
            pltpu.VMEM((CHUNKS * (LEV - 1) * 4 * per_level, bs, 2 * bs), BF16),
            pltpu.VMEM((CHUNKS, per_level * bs, bs), F32),
            pltpu.SemaphoreType.DMA((LEV, 4)),
            pltpu.SemaphoreType.DMA((LEV * CHUNKS, per_level)),
            pltpu.SemaphoreType.DMA((items, 6)),
            pltpu.SemaphoreType.DMA((items, 6)),
        ],
        compiler_params=pltpu.CompilerParams(collective_id=0, has_side_effects=True, vmem_limit_bytes=56 << 20),
        name="section_solve",
    )(pattern, right_sides, diag_inverse, coupling, off_blocks)


def scan_kernel(y_all, w_all, last_out, y_row, w_row, first, state, pair, xs, zs, in_sem, send_sem, recv_sem):
    sec, col = lax.axis_index("sec"), lax.axis_index("col")
    core = lax.rem(sec, 2)
    x = lax.rem(sec // 2, 4)
    z = sec // 8
    bs = w_row.shape[0]
    quarter = y_row.shape[1] // 4
    own_rows, map_rows = pl.ds(0, quarter), pl.ds(quarter, bs)

    def at(axis, step):
        if axis == "y":
            return {"col": lax.rem(col + step, 4)}
        if axis == "core":
            return {"sec": sec + 1 - 2 * core}
        if axis == "x":
            return {"sec": (z * 4 + lax.rem(x + step, 4)) * 2 + core}
        return {"sec": (lax.rem(z + step, 4) * 4 + x) * 2 + core}

    partners = [(axis, step) for axis in ("y", "x", "z") for step in (1, 2, 3)] + [("core", 1)]
    barrier = pltpu.get_barrier_semaphore()
    for axis, step in partners:
        pl.semaphore_signal(barrier, inc=1, device_id=at(axis, step), device_id_type=MESH)
    last_row = y_all.shape[0] - 1
    fetch = [pltpu.make_async_copy(y_all.at[last_row], y_row, in_sem.at[0]), pltpu.make_async_copy(w_all.at[last_row], w_row, in_sem.at[1])]
    for copy in fetch:
        copy.start()
    for copy in fetch:
        copy.wait()
    pl.semaphore_wait(barrier, len(partners))

    def remote(source, target, phase, axis, step):
        return pltpu.make_async_remote_copy(
            src_ref=source, dst_ref=target, send_sem=send_sem.at[phase, step], recv_sem=recv_sem.at[phase, step],
            device_id=at(axis, step), device_id_type=MESH,
        )

    shares = [remote(first.at[lax.rem(col + step, 4)], state, 0, "y", step) for step in (1, 2, 3)]

    @pl.when(col == 3)
    def _():
        map_t = w_row[...].T
        base_t = y_row[...].T
        for part in range(4):
            first[part, :quarter] = base_t[part * quarter : (part + 1) * quarter]
            first[part, quarter:] = map_t
        for copy in shares:
            copy.start()
        state[...] = first[3]
        for copy in shares:
            copy.wait_send()

    for part in range(3):

        @pl.when(col == part)
        def _(part=part):
            shares[part].wait_recv()

    def then(earlier, later):
        product = dot3(earlier, later[quarter:])
        return jnp.concatenate([product[:quarter] + later[:quarter], product[quarter:]], axis=0)

    swap = remote(state, pair, 1, "core", 1)
    swap.start()
    swap.wait()
    mine, other = state[...], pair[...]
    even = jnp.where(core == 0, mine, other)
    odd = jnp.where(core == 0, other, mine)
    both = then(even, odd)

    def spread(buffer, place, phase, axis, value):
        buffer[place] = value
        copies = [remote(buffer.at[place], buffer.at[place], phase, axis, step) for step in (1, 2, 3)]
        for copy in copies:
            copy.start()
        for step in (1, 2, 3):
            source = buffer.at[lax.rem(place + 4 - step, 4)]
            remote(source, source, phase, axis, step).wait_recv()
        return copies

    started = spread(xs, x, 2, "x", both)
    total = xs[0]
    before = jnp.where(x == 1, total, jnp.zeros_like(total))
    for place in (1, 2, 3):
        total = then(total, xs[place])
        if place < 3:
            before = jnp.where(x == place + 1, total, before)
    started += spread(zs, z, 3, "z", total)
    carried = zs[0][:quarter]
    incoming = jnp.where(z == 1, carried, jnp.zeros_like(carried))
    for place in (1, 2):
        carried = dot3(carried, zs[place][quarter:]) + zs[place][:quarter]
        incoming = jnp.where(z == place + 1, carried, incoming)
    through = jnp.where(x == 0, incoming, dot3(incoming, before[quarter:]) + before[:quarter])
    through = jnp.where(core == 0, through, dot3(through, even[quarter:]) + even[:quarter])
    started += spread(last_out, col, 4, "y", through)
    for copy in started:
        copy.wait_send()


def section_scan(solved, maps):
    rows, bs, width = solved.shape
    any_space = pl.BlockSpec(memory_space=pl.ANY)
    quarter = width // 4
    return pl.pallas_call(
        scan_kernel,
        out_shape=jax.ShapeDtypeStruct((4, quarter, bs), F32),
        in_specs=[any_space, any_space],
        out_specs=pl.BlockSpec(memory_space=pltpu.VMEM),
        scratch_shapes=[
            pltpu.VMEM((bs, width), F32),
            pltpu.VMEM((bs, bs), F32),
            pltpu.VMEM((4, quarter + bs, bs), F32),
            pltpu.VMEM((quarter + bs, bs), F32),
            pltpu.VMEM((quarter + bs, bs), F32),
            pltpu.VMEM((4, quarter + bs, bs), F32),
            pltpu.VMEM((4, quarter + bs, bs), F32),
            pltpu.SemaphoreType.DMA((2,)),
            pltpu.SemaphoreType.DMA((5, 4)),
            pltpu.SemaphoreType.DMA((5, 4)),
        ],
        compiler_params=pltpu.CompilerParams(collective_id=1, has_side_effects=True),
        name="section_scan",
    )(solved, maps)


def per_device(right_sides, diag_inverse, coupling, off_blocks, pattern):
    solved, maps = section_solve(right_sides[0, 0], diag_inverse[0, 0], coupling[0, 0], off_blocks[0, 0], pattern[0, 0])
    last = section_scan(solved, maps)
    last = last.reshape(-1, last.shape[-1])
    result = solved + jnp.einsum("pab,wb->paw", maps, last, precision=lax.Precision.HIGH)
    return result[None, None]


def solution(mesh):
    return jax.shard_map(
        per_device,
        mesh=mesh,
        in_specs=(
            P("sec", "col", None, None, None),
            P("sec", "col", None, None, None),
            P("sec", "col", None, None, None),
            P("sec", "col", None, None, None, None),
            P("sec", "col", None, None),
        ),
        out_specs=P("sec", "col", None, None, None),
        check_vma=False,
    )
```

time: 679 us -> 145 us (0.21)
  the two profiles are of different devices: /device:TPU:32 before, /device:TPU:0 now
where the time goes in v1:
time: 145 us; the launch traced here: 144 us
  Pallas kernels  139 us (96%)
  matrix products  4.01 us (3%)
    pallas_call x1, Pallas kernels, section_solve(): pl.pallas_call(section_kernel, out_shape=(jax.ShapeDtypeStruct((rows, bs,...  108 us
    pallas_call x1, Pallas kernels, section_scan(): pl.pallas_call(scan_kernel, out_shape=jax.ShapeDtypeStruct((4, quarter, b...  31.4 us
    dot_general x1, matrix products, per_device(): jnp.einsum('pab,wb->paw', maps, last, precision=lax.Precision.HIGH)  4.01 us

profile of v1, /device:TPU:0, one launch (start us, length us, event | category | flops | bytes accessed | tf_op | source)
XLA Modules:
  0.0 144.3 jit_solution(11518176579692999045)
XLA Ops:
  0.0 1.3 copy.8
  1.3 107.6 %section_solve.1 = (f32[20,128,256]{2,1,0:T(8,128)}, f32[20,128,128]{2,1,0:T(8,128)}) custom-call(s32[15,16]{1,0:T(8,128)} %bitcast.19, f32[20,128,256]{2,1,0:T(8,128)} %bitcast.15, f32[20,128,128]{2,1,0:T(8,128)} %bitcast.16, f32[20,128,128]{2,1,0:T(8,128)} %bitcast.17, f32[15,16,128,128]{3,2,1,0:T(8,128)} %bitcast.14), custom_call_target="tpu_custom_call" | custom-call | tf_op jit(solution)/shard_map/section_solve/pallas_call | solution.py:185
  108.9 0.0 copy-start
  108.9 31.4 %section_scan.1 = f32[4,64,128]{2,1,0:T(8,128)} custom-call(f32[20,128,256]{2,1,0:T(8,128)} %get-tuple-element.7.y_all, f32[20,128,128]{2,1,0:T(8,128)} %get-tuple-element.8.w_all), custom_call_target="tpu_custom_call" | custom-call | tf_op jit(solution)/shard_map/section_scan/pallas_call | solution.py:311
  140.3 0.0 copy-done
  140.3 4.0 %add_bitcast_fusion = f32[1,1,20,128,256]{4,3,2,1,0:T(8,128)} fusion(f32[20,128,256]{2,1,0:T(8,128)S(1)} %copy-done, f32[20,128,128]{2,1,0:T(8,128)} %get-tuple-element.8.w_all, f32[256,128,1]{1,0,2:T(8,128)} %bitcast.18), kind=kOutput, calls=%fused_computation | convolution fusion | flops 503971840 | bytes 6684672 | tf_op jit(solution)/shard_map/pab,wb->paw/dot_general | solution.py:337
Async XLA Ops:
  108.9 31.4 %copy-start = (f32[20,128,256]{2,1,0:T(8,128)S(1)}, f32[20,128,256]{2,1,0:T(8,128)}, u32[]{:S(2)}) copy-start(f32[20,128,256]{2,1,0:T(8,128)} %get-tuple-element.7.y_all) | copy-start | bytes 7864324
